TPU v7x, 512 devices: a whole 4x8x8 slice. The times are simulated.
512 devices in a mesh: bead: 32 (over z, x), space: 16 (over y, core).
Axes of the slice: x: 4, y: 8, z: 8, core: 2. Of those that a mesh axis runs over, the one named last changes fastest.
Arguments:
- positions: float32 [32, 3, 65536], P('bead', None, 'space'), may hold values from -5 to 5
- momenta: float32 [32, 3, 65536], P('bead', None, 'space'), may hold values from -6 to 6
- forces: float32 [32, 3, 65536], P('bead', None, 'space'), may hold values from -6 to 6
- noise: float32 [32, 3, 65536], P('bead', None, 'space'), may hold values from -6 to 6
- species: int32 [65536], P('space'), may hold values from 0 to 3
- block_pairs: int32 [2, 16384], P(None, 'space'), may hold values from 0 to 71, as said below
- pair_count: int32 [16], P('space'), may hold values from 128 to 1024, as said below
- halo_blocks: int32 [2, 64], P(None, 'space'), may hold values from 0 to 63, as said below
Outputs:
- positions_new: float32 [32, 3, 65536], P('bead', None, 'space')
- momenta_new: float32 [32, 3, 65536], P('bead', None, 'space')
- forces_new: float32 [32, 3, 65536], P('bead', None, 'space')
Inputs may be any that keep to these rules, and one draw needn't show every extreme that they name: `block_pairs`: columns 1024 * s to 1024 * (s + 1) - 1 belong to shard s; row 0 is a local block number below 64, row 1 an extended block number of that shard. `pair_count`: some shard uses all 1024 slots. `halo_blocks`: columns 4 * s to 4 * (s + 1) - 1 belong to shard s; the 8 numbers of a shard are distinct local block numbers.
All inputs are finite; a program needn't handle non-finite values.
Results may differ from a plain program's by a relative error of at most 0.0003.
Values sent between devices are 32-bit elements; how exact they have to be, the bound alone decides.
A program may use at most 64 MiB of HBM per device.

v0:
```python
import jax
import jax.numpy as jnp
from jax import lax
from jax.sharding import PartitionSpec as P

BLOCK = 64
eps_pair = 0.01
time_step = 0.5
gamma_centroid = 0.5
pair_group = 16
mass_values = (1.0, 0.3, 2.5, 0.75)
strength_values = (1.0, 0.5, 1.5, 0.8)
reach_values = (1.0, 0.6, 1.4, 0.9)
highest = lax.Precision.HIGHEST


def with_halo(cells, sides, width):
    for axis, dim in sides:
        count = lax.axis_size(axis)
        ends = count - 1
        head = lax.slice_in_dim(cells, 0, width, axis=dim)
        tail = lax.slice_in_dim(cells, cells.shape[dim] - width, cells.shape[dim], axis=dim)
        cells = jnp.concatenate(
            [
                lax.ppermute(tail, axis, [(i, (i + 1) % count) for i in range(ends)]),
                cells,
                lax.ppermute(head, axis, [((i + 1) % count, i) for i in range(ends)]),
            ],
            axis=dim,
        )
    return cells


def lookup(values_list, species):
    result = jnp.zeros(species.shape, jnp.float32)
    for species_kind in range(4):
        result = result + jnp.where(species == species_kind, values_list[species_kind], 0.0).astype(
            jnp.float32
        )
    return result


def modes_matrix(bead_count):
    steps_int = jnp.arange(bead_count, dtype=jnp.int32)
    product_mod = steps_int[:, None] * steps_int[None, :] % bead_count
    phase_angle = 2.0 * jnp.pi * product_mod.astype(jnp.float32) / bead_count
    mode_grid = jnp.broadcast_to(steps_int[None, :], (bead_count, bead_count))
    bead_grid = jnp.broadcast_to(steps_int[:, None], (bead_count, bead_count))
    half_modes = bead_count // 2
    root_one = jnp.sqrt(jnp.float32(1.0 / bead_count))
    root_two = jnp.sqrt(jnp.float32(2.0 / bead_count))
    matrix = jnp.where(
        mode_grid < half_modes, root_two * jnp.cos(phase_angle), root_two * jnp.sin(phase_angle)
    )
    matrix = jnp.where(mode_grid == 0, root_one, matrix)
    alternating = jnp.where(bead_grid % 2 == 0, root_one, -root_one)
    matrix = jnp.where(mode_grid == half_modes, alternating, matrix)
    return matrix


def propagate(q_modes, p_modes, noise_modes, masses, mode_numbers, bead_count):
    mode_float = mode_numbers.astype(jnp.float32)[:, None, None]
    centroid = (mode_numbers == 0)[:, None, None]
    frequency = 2.0 * jnp.sin(jnp.pi * mode_float / bead_count)
    friction = jnp.where(centroid, gamma_centroid, 2.0 * frequency)
    damping = jnp.exp(-friction * time_step)
    spread = jnp.sqrt(1.0 - damping * damping)
    p_mixed = damping * p_modes + spread * jnp.sqrt(masses) * noise_modes
    safe_freq = jnp.where(centroid, 1.0, frequency)
    cosine = jnp.cos(frequency * time_step)
    sine_term = jnp.sin(frequency * time_step)
    q_cycle = cosine * q_modes + sine_term / (masses * safe_freq) * p_mixed
    p_cycle = -masses * safe_freq * sine_term * q_modes + cosine * p_mixed
    q_next = jnp.where(centroid, q_modes + time_step * p_mixed / masses, q_cycle)
    p_next = jnp.where(centroid, p_mixed, p_cycle)
    return (q_next, p_next)


def group_force(pos_i, pos_j, par_i, par_j, live_mask):
    pair_width = par_i[1][:, :, None] + par_j[1][:, None, :]
    weight_base = (
        eps_pair
        * 2.0
        * par_i[0][:, :, None]
        * par_j[0][:, None, :]
        / pair_width
        * live_mask[:, None, None]
    )
    norm_i = jnp.sum(pos_i * pos_i, axis=1)
    norm_j = jnp.sum(pos_j * pos_j, axis=1)
    cross_term = jnp.einsum("bcgi,bcgj->bgij", pos_i, pos_j, precision=highest)
    distance = norm_i[..., :, None] + norm_j[..., None, :] - 2.0 * cross_term
    weight = weight_base[None] * jnp.exp(-distance / pair_width[None])
    weight_sum = jnp.sum(weight, axis=3)
    pulled = jnp.einsum("bgij,bcgj->bcgi", weight, pos_j, precision=highest)
    return pos_i * weight_sum[:, None] - pulled


def shards(positions, momenta, forces, noise, species, block_pairs, pair_count, halo_blocks):
    local_beads = positions.shape[0]
    bead_count = local_beads * lax.axis_size("bead")
    atoms_here = positions.shape[2]
    masses = lookup(mass_values, species)
    strength = lookup(strength_values, species)
    reach = lookup(reach_values, species)
    matrix = modes_matrix(bead_count)
    p_half = momenta + 0.5 * time_step * forces
    first_bead = lax.axis_index("bead") * local_beads
    my_cols = lax.dynamic_slice_in_dim(matrix, first_bead, local_beads, 1)
    my_rows = lax.dynamic_slice_in_dim(matrix, first_bead, local_beads, 0)
    my_modes = first_bead + jnp.arange(local_beads, dtype=jnp.int32)
    pieces = (
        lax.all_gather(positions, "bead", axis=0, tiled=True),
        lax.all_gather(p_half, "bead", axis=0, tiled=True),
    )
    q_modes = jnp.einsum("jk,jcn->kcn", my_cols, pieces[0], precision=highest)
    p_modes = jnp.einsum("jk,jcn->kcn", my_cols, pieces[1], precision=highest)
    q_next, p_next = propagate(q_modes, p_modes, noise, masses, my_modes, bead_count)
    pieces = (
        lax.all_gather(q_next, "bead", axis=0, tiled=True),
        lax.all_gather(p_next, "bead", axis=0, tiled=True),
    )
    positions_new = jnp.einsum("jk,kcn->jcn", my_rows, pieces[0], precision=highest)
    p_mid = jnp.einsum("jk,kcn->jcn", my_rows, pieces[1], precision=highest)
    block_total = atoms_here // BLOCK
    halo_count = halo_blocks.shape[1]
    halo_width = halo_count * BLOCK
    coord_rows = local_beads * 3
    all_rows = jnp.concatenate(
        [positions_new.reshape(coord_rows, atoms_here), jnp.stack([strength, reach])], axis=0
    )
    row_total = all_rows.shape[0]
    outgoing = jnp.take(
        all_rows.reshape(row_total, block_total, BLOCK), halo_blocks.reshape(-1), axis=1
    ).reshape(row_total, 2 * halo_width)
    padded = with_halo(outgoing, (("space", 1),), halo_width)
    extended = jnp.concatenate(
        [padded[:, :halo_width], all_rows, padded[:, padded.shape[1] - halo_width :]], axis=1
    )
    extended = extended.reshape(row_total, block_total + 2 * halo_count, BLOCK)
    live_count = pair_count[0]
    group_count = (live_count + pair_group - 1) // pair_group

    def add_group(group, totals):
        pair_ids = lax.dynamic_slice_in_dim(block_pairs, group * pair_group, pair_group, 1)
        slots = group * pair_group + jnp.arange(pair_group, dtype=jnp.int32)
        live_mask = (slots < live_count).astype(jnp.float32)
        take_i = jnp.take(extended, pair_ids[0] + halo_count, axis=1)
        take_j = jnp.take(extended, pair_ids[1], axis=1)
        pos_i = take_i[:coord_rows].reshape(local_beads, 3, pair_group, BLOCK)
        pos_j = take_j[:coord_rows].reshape(local_beads, 3, pair_group, BLOCK)
        force_part = group_force(pos_i, pos_j, take_i[coord_rows:], take_j[coord_rows:], live_mask)
        one_hot = (
            pair_ids[0][:, None] == jnp.arange(block_total, dtype=jnp.int32)[None, :]
        ).astype(jnp.float32)
        return totals + jnp.einsum("bcgi,gk->bcki", force_part, one_hot, precision=highest)

    force_start = jnp.zeros((local_beads, 3, block_total, BLOCK), jnp.float32)
    forces_new = lax.fori_loop(0, group_count, add_group, force_start).reshape(
        local_beads, 3, atoms_here
    )
    momenta_new = p_mid + 0.5 * time_step * forces_new
    return (positions_new, momenta_new, forces_new)


def solution(mesh):
    in_specs = (
        P("bead", None, "space"),
        P("bead", None, "space"),
        P("bead", None, "space"),
        P("bead", None, "space"),
        P("space"),
        P(None, "space"),
        P("space"),
        P(None, "space"),
    )
    out_specs = (P("bead", None, "space"), P("bead", None, "space"), P("bead", None, "space"))
    return jax.shard_map(shards, mesh=mesh, in_specs=in_specs, out_specs=out_specs, check_vma=False)
```

profile of v0, /device:TPU:40, one launch (start us, length us, event | category | flops | bytes accessed | tf_op | source)
XLA Modules:
  0.0 699.7 jit_solution(3342020693959065809)
XLA Ops:
  11.6 87.8 %all-gather.5.cloned.1.call-done = f32[32,3,4096]{2,1,0:T(4,128)} async-done(((f32[1,3,4096]{2,1,0:T(4,128)}), f32[32,3,4096]{2,1,0:T(4,128)}) %all-gather.5.cloned.1.call-update) | async-done | bytes 1572880 | tf_op jit(solution)/shard_map/all_gather | solution.py:113
  99.4 3.2 fusion.22
  102.7 80.8 %all-gather.7.cloned.1.call-done = f32[32,3,4096]{2,1,0:T(4,128)} async-done(((f32[1,3,4096]{2,1,0:T(4,128)}), f32[32,3,4096]{2,1,0:T(4,128)}) %all-gather.7.cloned.1.call-update) | async-done | bytes 1572880 | tf_op jit(solution)/shard_map/all_gather | solution.py:114
  183.5 3.2 fusion.20
  189.5 79.0 %all-gather.9.cloned.1.call-done = f32[32,3,4096]{2,1,0:T(4,128)} async-done(((f32[1,3,4096]{2,1,0:T(4,128)}), f32[32,3,4096]{2,1,0:T(4,128)}) %all-gather.9.cloned.1.call-update) | async-done | bytes 1572880 | tf_op jit(solution)/shard_map/all_gather | solution.py:120
  268.5 3.2 fusion.18
  272.8 1.9 collective-permute-start
  274.7 3.6 collective-permute-start.1
  278.3 74.0 %all-gather.11.cloned.1.call-done = f32[32,3,4096]{2,1,0:T(4,128)} async-done(((f32[1,3,4096]{2,1,0:T(4,128)}), f32[32,3,4096]{2,1,0:T(4,128)}) %all-gather.11.cloned.1.call-update) | async-done | bytes 1572880 | tf_op jit(solution)/shard_map/all_gather | solution.py:121
  352.4 3.2 fusion.16
  356.5 335.1 %while.10 = (s32[]{:T(128)}, f32[1,3,64,64]{3,2,1,0:T(8,128)S(1)}, s32[]{:T(128)}, s32[2,1024]{1,0:T(2,128)}, f32[5,72,64]{2,0,1:T(8,128)S(1)}, /*index=5*/s32[]...) while((s32[]{:T(128)}, f32[1,3,64,64]{3,2,1,0:T(8,128)S(1)}, s32[]{:T(128)}, s32[2,1024]{1,0:T(2,128)}, ...), condition=%wide.region_4.6_spmd, body=%wide.region_0.5_spmd.sunk | while | flops 7841030 | bytes 1341151 | solution.py:159
  369.9 1.5 fusion.66
  375.1 1.5 fusion.66
  390.8 1.5 fusion.66
  396.0 1.5 fusion.66
  411.7 1.5 fusion.66
  448.4 1.5 fusion.66
  464.1 1.5 fusion.66
  469.3 1.5 fusion.66
  485.0 1.5 fusion.66
  490.3 1.5 fusion.66
  506.0 1.5 fusion.66
  537.4 1.5 fusion.66
  542.6 1.5 fusion.66
  (1063 shorter events, 317.6 us)
Async XLA Ops:
  7.2 179.5 %copy-start = (f32[1,3,4096]{2,0,1:T(1,128)S(1)}, f32[1,3,4096]{2,0,1:T(1,128)}, u32[]{:S(2)}) copy-start(f32[1,3,4096]{2,0,1:T(1,128)} %param.15) | copy-start | bytes 147460
  7.2 92.2 %all-gather.5.cloned.1.call-start = ((), (), s32[]{:S(2)}) async-start(), calls=%async_computation | async-start | bytes 2162688 | tf_op jit(solution)/shard_map/all_gather | solution.py:113
  8.7 180.0 %copy-start.1 = (s32[2,4]{1,0:T(2,128)S(1)}, s32[2,4]{1,0:T(2,128)}, u32[]{:S(2)}) copy-start(s32[2,4]{1,0:T(2,128)} %param.19) | copy-start | bytes 100
  8.7 174.7 %all-gather.7.cloned.1.call-start = ((), (), s32[]{:S(2)}) async-start(), calls=%async_computation.1 | async-start | bytes 2162688 | tf_op jit(solution)/shard_map/all_gather | solution.py:114
  10.3 258.2 %all-gather.9.cloned.1.call-start = ((), (), s32[]{:S(2)}) async-start(), calls=%async_computation.2 | async-start | bytes 2162688 | tf_op jit(solution)/shard_map/all_gather | solution.py:120
  187.5 164.9 %all-gather.11.cloned.1.call-start = ((), (), s32[]{:S(2)}) async-start(), calls=%async_computation.3 | async-start | bytes 2162688 | tf_op jit(solution)/shard_map/all_gather | solution.py:121
  272.8 83.5 %collective-permute-start = (f32[5,256]{1,0:T(8,128)S(1)}, f32[5,256]{1,0:T(8,128)S(1)}, u32[]{:S(2)}, u32[]{:S(2)}) collective-permute-start(f32[5,256]{1,0:T(8,128)S(1)} %get-tuple-element.89), channel_id=1, source_target_pairs={{0,1},{1,2},{2,3},{3,4},{4,5},{5,6},{6,7},{7,8},{8,9},{9,10},{10,1... | collective-permute-start | bytes 15368 | tf_op jit(solution)/shard_map/ppermute | solution.py:25
  274.7 81.6 %collective-permute-start.1 = (f32[5,256]{1,0:T(8,128)S(1)}, f32[5,256]{1,0:T(8,128)S(1)}, u32[]{:S(2)}, u32[]{:S(2)}) collective-permute-start(f32[5,256]{1,0:T(8,128)S(1)} %get-tuple-element.90), channel_id=1, source_target_pairs={{1,0},{2,1},{3,2},{4,3},{5,4},{6,5},{7,6},{8,7},{9,8},{10,9},{11,1... | collective-permute-start | bytes 15368 | tf_op jit(solution)/shard_map/ppermute | solution.py:27
Sparse Core Ops, SparseCore 0:
  11.2 88.2 all-gather.4
  102.6 80.8 all-gather.6
  187.6 80.8 all-gather.8
  271.5 80.8 all-gather.10
where the time goes:
time: 702 us; the launch traced here: 700 us
  waiting for transfers between devices  322 us (46%)
  matrix products  165 us (24%)
  local copies, waits for them, and re-layouts  127 us (18%)
  other arithmetic  57.5 us (8%)
  between operations  15 us (2%)
  loops' own time  7.25 us (1%)
    dot_general x64, matrix products, group_force(): cross_term = jnp.einsum('bcgi,bcgj->bgij', pos_i, pos_j, precision=highest)  96.6 us
    all_gather x1, waiting for transfers between devices, shards(): lax.all_gather(positions, 'bead', axis=0, tiled=True)  87.8 us
    all_gather x1, waiting for transfers between devices, shards(): lax.all_gather(p_half, 'bead', axis=0, tiled=True)  80.8 us
    all_gather x1, waiting for transfers between devices, shards(): lax.all_gather(q_next, 'bead', axis=0, tiled=True)  79 us
    all_gather x1, waiting for transfers between devices, shards(): lax.all_gather(p_next, 'bead', axis=0, tiled=True)  74 us
    dynamic_slice x64, local copies, waits for them, and re-layouts, add_group(): lax.dynamic_slice_in_dim(block_pairs, group * pair_group, pair_group, 1)  48.4 us
    convert_element_type x64, other arithmetic, add_group(): live_mask = (slots < live_count).astype(jnp.float32)  41.7 us
    gather x64, local copies, waits for them, and re-layouts, add_group(): take_j = jnp.take(extended, pair_ids[1], axis=1)  36.2 us
  transfers between devices with their start and end apart: 6, of which 4 were waited for; matrix products, arithmetic and copies ran while one was open for 2% of the time, Pallas kernels for 0%

commit v1 on v0

--- a/solution.py
+++ b/solution.py
@@ -111,7 +111,9 @@
     my_modes = first_bead + jnp.arange(local_beads, dtype=jnp.int32)
     pieces = (
         lax.all_gather(positions, "bead", axis=0, tiled=True),
-        lax.all_gather(p_half, "bead", axis=0, tiled=True),
+        jnp.concatenate(
+            lax.all_to_all(jnp.stack([p_half] * lax.axis_size("bead")), "bead", 0, 0), axis=0
+        ),
     )
     q_modes = jnp.einsum("jk,jcn->kcn", my_cols, pieces[0], precision=highest)
     p_modes = jnp.einsum("jk,jcn->kcn", my_cols, pieces[1], precision=highest)

time: 702 us -> 634 us (0.903)
  waiting for transfers between devices: 322 us -> 242 us
  starting transfers between devices: 5.72 us -> 19 us
    all_gather x1 -> x0, waiting for transfers between devices: 80.8 us -> none  [shards(): lax.all_gather(p_half, 'bead', axis=0, tiled=True)]
    all_gather x1, waiting for transfers between devices: 87.8 us -> 48.9 us  [shards(): lax.all_gather(positions, 'bead', axis=0, tiled=True)]
    all_to_all x0 -> x1, waiting for transfers between devices: none -> 38.9 us  [shards(): lax.all_to_all(jnp.stack([p_half] * lax.axis_size('bead')), 'bead', 0, 0)]
    all_to_all x0 -> x1, starting transfers between devices: none -> 13.3 us  [shards(): lax.all_to_all(jnp.stack([p_half] * lax.axis_size('bead')), 'bead', 0, 0)]
where the time goes in v1:
time: 634 us; the launch traced here: 632 us
  waiting for transfers between devices  242 us (38%)
  matrix products  163 us (26%)
  local copies, waits for them, and re-layouts  129 us (20%)
  other arithmetic  56.3 us (9%)
  starting transfers between devices  19 us (3%)
  between operations  15 us (2%)
  loops' own time  7.52 us (1%)
    dot_general x64, matrix products, group_force(): cross_term = jnp.einsum('bcgi,bcgj->bgij', pos_i, pos_j, precision=highest)  96.6 us
    all_gather x1, waiting for transfers between devices, shards(): lax.all_gather(q_next, 'bead', axis=0, tiled=True)  78.9 us
    all_gather x1, waiting for transfers between devices, shards(): lax.all_gather(p_next, 'bead', axis=0, tiled=True)  74.2 us
    all_gather x1, waiting for transfers between devices, shards(): lax.all_gather(positions, 'bead', axis=0, tiled=True)  48.9 us
    dynamic_slice x64, local copies, waits for them, and re-layouts, add_group(): lax.dynamic_slice_in_dim(block_pairs, group * pair_group, pair_group, 1)  48.3 us
    convert_element_type x64, other arithmetic, add_group(): live_mask = (slots < live_count).astype(jnp.float32)  41.7 us
    all_to_all x1, waiting for transfers between devices, shards(): lax.all_to_all(jnp.stack([p_half] * lax.axis_size('bead')), 'bead', 0, 0)  38.9 us
    gather x64, local copies, waits for them, and re-layouts, add_group(): take_j = jnp.take(extended, pair_ids[1], axis=1)  36.2 us
  transfers between devices with their start and end apart: 6, of which 4 were waited for; matrix products, arithmetic and copies ran while one was open for 2% of the time, Pallas kernels for 0%

profile of v1, /device:TPU:40, one launch (start us, length us, event | category | flops | bytes accessed | tf_op | source)
XLA Modules:
  0.0 631.5 jit_solution(207098700220926440)
XLA Ops:
  8.1 2.7 stack.6
  10.8 13.3 %all-to-all-start = ((f32[32,1,3,4096]{3,1,2,0:T(1,128)}), f32[32,1,3,4096]{3,1,2,0:T(1,128)S(1)}, u32[]{:S(2)}, u32[]{:S(2)}) async-start(f32[32,1,3,4096]{3,1,2,0:T(1,128)} %stack.6), calls=%async_computation | async-start | bytes 3145728 | tf_op jit(solution)/shard_map/all_to_all | solution.py:115
  25.5 38.9 %all-to-all-done = f32[32,1,3,4096]{3,1,2,0:T(1,128)S(1)} async-done(((f32[32,1,3,4096]{3,1,2,0:T(1,128)}), f32[32,1,3,4096]{3,1,2,0:T(1,128)S(1)}, u32[]{:S(2)}, u32[]{:S(2)}) %all-to-all-start) | async-done | bytes 1572896 | tf_op jit(solution)/shard_map/all_to_all | solution.py:115
  64.4 1.7 fusion.16
  66.1 48.9 %all-gather.4.cloned.1.call-done = f32[32,3,4096]{2,1,0:T(4,128)} async-done(((f32[1,3,4096]{2,1,0:T(4,128)}), f32[32,3,4096]{2,1,0:T(4,128)}) %all-gather.4.cloned.1.call-update) | async-done | bytes 1572880 | tf_op jit(solution)/shard_map/all_gather | solution.py:113
  115.0 3.2 fusion.22
  121.2 78.9 %all-gather.6.cloned.1.call-done = f32[32,3,4096]{2,1,0:T(4,128)} async-done(((f32[1,3,4096]{2,1,0:T(4,128)}), f32[32,3,4096]{2,1,0:T(4,128)}) %all-gather.6.cloned.1.call-update) | async-done | bytes 1572880 | tf_op jit(solution)/shard_map/all_gather | solution.py:122
  200.0 3.2 fusion.20
  204.3 1.9 collective-permute-start
  206.2 3.6 collective-permute-start.1
  209.9 74.2 %all-gather.8.cloned.1.call-done = f32[32,3,4096]{2,1,0:T(4,128)} async-done(((f32[1,3,4096]{2,1,0:T(4,128)}), f32[32,3,4096]{2,1,0:T(4,128)}) %all-gather.8.cloned.1.call-update) | async-done | bytes 1572880 | tf_op jit(solution)/shard_map/all_gather | solution.py:123
  284.1 3.2 fusion.18
  288.2 335.2 %while.10 = (s32[]{:T(128)}, f32[1,3,64,64]{3,2,1,0:T(8,128)S(1)}, s32[]{:T(128)}, s32[2,1024]{1,0:T(2,128)}, f32[5,72,64]{2,0,1:T(8,128)S(1)}, /*index=5*/s32[]...) while((s32[]{:T(128)}, f32[1,3,64,64]{3,2,1,0:T(8,128)S(1)}, s32[]{:T(128)}, s32[2,1024]{1,0:T(2,128)}, ...), condition=%wide.region_4.6_spmd, body=%wide.region_0.5_spmd.sunk | while | flops 7841030 | bytes 1341151 | solution.py:161
  291.0 1.5 fusion.67
  306.8 1.5 fusion.67
  312.0 1.5 fusion.67
  327.7 1.5 fusion.67
  332.9 1.5 fusion.67
  348.7 1.5 fusion.67
  369.6 1.5 fusion.67
  390.6 1.5 fusion.67
  406.3 1.5 fusion.67
  411.5 1.5 fusion.67
  427.2 1.5 fusion.67
  (1068 shorter events, 318.6 us)
Async XLA Ops:
  10.8 13.4 %copy-start = (f32[1,3,4096]{2,0,1:T(1,128)S(1)}, f32[1,3,4096]{2,0,1:T(1,128)}, u32[]{:S(2)}) copy-start(f32[1,3,4096]{2,0,1:T(1,128)} %param.12) | copy-start | bytes 147460
  10.8 14.6 %copy-start.2 = (s32[4096]{0:T(1024)S(1)}, s32[4096]{0:T(1024)}, u32[]{:S(2)}) copy-start(s32[4096]{0:T(1024)} %param.16) | copy-start | bytes 49156
  10.8 53.6 %all-to-all-start = ((f32[32,1,3,4096]{3,1,2,0:T(1,128)}), f32[32,1,3,4096]{3,1,2,0:T(1,128)S(1)}, u32[]{:S(2)}, u32[]{:S(2)}) async-start(f32[32,1,3,4096]{3,1,2,0:T(1,128)} %stack.6), calls=%async_computation | async-start | bytes 3145728 | tf_op jit(solution)/shard_map/all_to_all | solution.py:115
  24.1 90.9 %all-gather.4.cloned.1.call-start = ((), (), s32[]{:S(2)}) async-start(), calls=%async_computation.1 | async-start | bytes 2162688 | tf_op jit(solution)/shard_map/all_gather | solution.py:113
  24.8 175.2 %all-gather.6.cloned.1.call-start = ((), (), s32[]{:S(2)}) async-start(), calls=%async_computation.2 | async-start | bytes 2162688 | tf_op jit(solution)/shard_map/all_gather | solution.py:122
  25.4 92.8 %copy-start.1 = (f32[1,3,4096]{2,0,1:T(1,128)S(1)}, f32[1,3,4096]{2,0,1:T(1,128)}, u32[]{:S(2)}) copy-start(f32[1,3,4096]{2,0,1:T(1,128)} %param.15) | copy-start | bytes 147460
  25.4 94.3 %copy-start.3 = (s32[2,4]{1,0:T(2,128)S(1)}, s32[2,4]{1,0:T(2,128)}, u32[]{:S(2)}) copy-start(s32[2,4]{1,0:T(2,128)} %param.19) | copy-start | bytes 100
  119.0 165.0 %all-gather.8.cloned.1.call-start = ((), (), s32[]{:S(2)}) async-start(), calls=%async_computation.3 | async-start | bytes 2162688 | tf_op jit(solution)/shard_map/all_gather | solution.py:123
  204.3 83.7 %collective-permute-start = (f32[5,256]{1,0:T(8,128)S(1)}, f32[5,256]{1,0:T(8,128)S(1)}, u32[]{:S(2)}, u32[]{:S(2)}) collective-permute-start(f32[5,256]{1,0:T(8,128)S(1)} %get-tuple-element.95), channel_id=1, source_target_pairs={{0,1},{1,2},{2,3},{3,4},{4,5},{5,6},{6,7},{7,8},{8,9},{9,10},{10,1... | collective-permute-start | bytes 15368 | tf_op jit(solution)/shard_map/ppermute | solution.py:25
  206.2 81.8 %collective-permute-start.1 = (f32[5,256]{1,0:T(8,128)S(1)}, f32[5,256]{1,0:T(8,128)S(1)}, u32[]{:S(2)}, u32[]{:S(2)}) collective-permute-start(f32[5,256]{1,0:T(8,128)S(1)} %get-tuple-element.96), channel_id=1, source_target_pairs={{1,0},{2,1},{3,2},{4,3},{5,4},{6,5},{7,6},{8,7},{9,8},{10,9},{11,1... | collective-permute-start | bytes 15368 | tf_op jit(solution)/shard_map/ppermute | solution.py:27
Sparse Core Ops, SparseCore 0:
  28.1 86.8 all-gather.3
  119.1 80.8 all-gather.5
  203.2 80.8 all-gather.7
